TPU v7x, 512 devices: a whole 4x8x8 slice. The times are simulated.
512 devices in a mesh: rep: 64 (over y, x, z_hi), row: 8 (over z_lo, core).
Axes of the slice: x: 4, y: 8, z: 8 (z_hi: 2, z_lo: 4; z = z_hi * 4 + z_lo), core: 2. Of those that a mesh axis runs over, the one named last changes fastest.
Arguments:
- features: bfloat16 [64, 1, 48, 48, 2048], P('rep', None, 'row'), may hold values from -6 to 6
- weights: bfloat16 [64, 3, 3, 2048, 256], P('rep', None, None, 'row'), may hold values from -5 to 5
- upstream: bfloat16 [64, 1, 48, 48, 256], P('rep', None, 'row'), may hold values from -6 to 6
- step_index: int32 [1], replicated, may hold values from 0 to 1023
Outputs:
- new_weights: bfloat16 [64, 3, 3, 2048, 256], P('rep', None, None, 'row')
All inputs are finite; a program needn't handle non-finite values.
Results may differ from a plain program's by a relative error of at most 0.0027.
Values may be sent and summed in bfloat16 or wider, within the bound.
A program may use at most 64 MiB of HBM per device.

v0:
```python
from functools import partial

import jax
import jax.numpy as jnp
from jax import lax
from jax.sharding import PartitionSpec as P

R = 6
HOPS = 4


def from_behind(block, axis, distance):
    devices = range(lax.axis_size(axis))
    route = [((i - distance) % len(devices), i) for i in devices]
    return lax.ppermute(block, axis, route)


def with_halo(cells, sides, width):
    for axis, dim in sides:
        count = lax.axis_size(axis)
        ends = count - 1
        head = lax.slice_in_dim(cells, 0, width, axis=dim)
        tail = lax.slice_in_dim(cells, cells.shape[dim] - width, cells.shape[dim], axis=dim)
        cells = jnp.concatenate(
            [
                lax.ppermute(tail, axis, [(i, (i + 1) % count) for i in range(ends)]),
                cells,
                lax.ppermute(head, axis, [((i + 1) % count, i) for i in range(ends)]),
            ],
            axis=dim,
        )
    return cells


def silu_slope(value):
    sig = jax.nn.sigmoid(value)
    return sig * (1.0 + value * (1.0 - sig))


def hop_peer(distance, value):
    return from_behind(value, "rep", distance)


def per_device(features, weights, upstream, step_index):
    feats = features[0]
    kernel = weights[0]
    batch, rows_dev, cols, chans_in = feats.shape
    share = kernel.shape[2]
    chans_out = kernel.shape[3]
    rows_all = rows_dev * lax.axis_size("row")
    scale_in = 1.0 / jnp.sqrt(jnp.float32(9 * chans_in))
    scale_grad = 1.0 / jnp.sqrt(jnp.float32(batch * rows_all * cols))
    regrouped = lax.all_to_all(feats, "row", split_axis=3, concat_axis=1, tiled=True)
    own_pad = jnp.pad(regrouped, ((0, 0), (R, R), (R, R), (0, 0)))
    padded = with_halo(feats, (("row", 1),), R)
    padded = jnp.pad(padded, ((0, 0), (0, 0), (R, R), (0, 0)))
    empty = jnp.zeros((batch * rows_dev * cols, chans_out), jnp.float32)
    total = empty
    piece = lax.all_gather(kernel, "row", axis=2, tiled=True)
    count = piece.shape[2]
    for p in range(3):
        for q in range(3):
            win = padded[:, p * R : p * R + rows_dev, q * R : q * R + cols, :]
            win = win.reshape(-1, count)
            total = total + jnp.dot(win, piece[p, q], preferred_element_type=jnp.float32)
    pre = (total * scale_in).reshape(batch, rows_dev, cols, chans_out)
    slope = (upstream[0].astype(jnp.float32) * silu_slope(pre)).astype(jnp.bfloat16)
    piece = lax.all_gather(slope, "row", axis=1, tiled=True)
    height = piece.shape[1]
    flat = piece.reshape(-1, chans_out)
    terms = []
    for p in range(3):
        for q in range(3):
            win = lax.dynamic_slice_in_dim(own_pad, p * R, height, 1)
            win = win[:, :, q * R : q * R + cols, :].reshape(-1, share)
            terms.append(
                lax.dot_general(
                    win, flat, (((0,), (0,)), ((), ())), preferred_element_type=jnp.float32
                )
            )
    grad = jnp.stack(terms)
    grad = (grad * scale_grad).reshape(3, 3, share, chans_out)
    rate = 1.0 / jnp.sqrt(1.0 + step_index[0].astype(jnp.float32) / 1024.0)
    stepped = kernel.astype(jnp.float32) - rate * grad
    selector = step_index[0] % HOPS
    branches = [partial(hop_peer, 1 << k) for k in range(HOPS)]
    peer = lax.switch(selector, branches, stepped)
    averaged = ((stepped + peer) * 0.5).astype(jnp.bfloat16)
    return averaged[None]


def solution(mesh):
    in_specs = (
        P("rep", None, "row", None, None),
        P("rep", None, None, "row", None),
        P("rep", None, "row", None, None),
        P(),
    )
    out_specs = P("rep", None, None, "row", None)
    return jax.shard_map(
        per_device, mesh=mesh, in_specs=in_specs, out_specs=out_specs, check_vma=False
    )
```

profile of v0, /device:TPU:1, one launch (start us, length us, event | category | flops | bytes accessed | tf_op | source)
XLA Modules:
  0.0 269.7 jit_solution(1789089261947107116)
XLA Ops:
  6.5 0.0 copy-start.2
  6.5 0.0 all-gather.6.cloned.1.call-start
  6.5 0.7 all-gather.6.cloned.1.call-update
  7.3 0.5 copy-done.2
  7.8 5.4 %collective-permute-start.4 = (bf16[1,6,48,2048]{3,2,1,0:T(8,128)(2,1)S(1)}, bf16[1,6,48,2048]{3,2,1,0:T(8,128)(2,1)}, u32[]{:S(2)}, u32[]{:S(2)}) collective-permute-start(bf16[1,6,48,2048]{3,2,1,0:T(8,128)(2,1)S(1)} %bitcast.255), channel_id=1, source_target_pairs={{0,1},{1,2},{2,3},{3,4},{4,5},{5,6},{6,7},{8,9},{9,10},{10,11},{11... | collective-permute-start | bytes 3538952 | tf_op jit(solution)/shard_map/ppermute | solution.py:26
  13.2 5.7 %collective-permute-start.5 = (bf16[1,6,48,2048]{3,2,1,0:T(8,128)(2,1)S(1)}, bf16[1,6,48,2048]{3,2,1,0:T(8,128)(2,1)S(1)}, u32[]{:S(2)}, u32[]{:S(2)}) collective-permute-start(bf16[1,6,48,2048]{3,2,1,0:T(8,128)(2,1)S(1)} %bitcast.256), channel_id=1, source_target_pairs={{1,0},{2,1},{3,2},{4,3},{5,4},{6,5},{7,6},{9,8},{10,9},{11,10},{12... | collective-permute-start | bytes 3538952 | tf_op jit(solution)/shard_map/ppermute | solution.py:28
  18.9 4.2 %copy.12 = bf16[1,6,48,2048]{2,1,0,3:T(8,128)(2,1)} copy(bf16[1,6,48,2048]{3,2,1,0:T(8,128)(2,1)S(1)} %bitcast.257) | data formatting | bytes 2359296 | tf_op jit(solution)/shard_map/squeeze | solution.py:45
  23.1 8.1 %reshape.186 = bf16[8,2,36864]{2,1,0:T(2,128)(2,1)} reshape(bf16[2048,1,6,48]{3,2,1,0:T(8,128)(2,1)} %bitcast.251) | data formatting | bytes 2359296
  31.2 3.5 %all-to-all-start = ((bf16[8,2,36864]{2,1,0:T(2,128)(2,1)}), bf16[8,2,36864]{2,1,0:T(2,128)(2,1)S(1)}, u32[]{:S(2)}, u32[]{:S(2)}) async-start(bf16[8,2,36864]{2,1,0:T(2,128)(2,1)} %reshape.186), calls=%async_computation | async-start | bytes 2359296 | tf_op jit(solution)/shard_map/all_to_all | solution.py:53
  34.7 0.0 all-gather.4.cloned.1.call-start
  34.7 0.0 collective-permute-done.4
  34.7 0.0 collective-permute-done.5
  34.8 0.0 copy-start.7
  34.8 1.1 copy-done.7
  35.8 2.9 %fusion.5 = bf16[1,18,60,2048]{3,2,1,0:T(8,128)(2,1)S(1)} fusion(bf16[1,6,48,2048]{3,2,1,0:T(8,128)(2,1)S(1)} %collective-permute-done.5, bf16[1,6,48,2048]{3,2,1,0:T(8,128)(2,1)S(1)} %bitcast.258, bf16[1,6,48,2048]{3,2,1,0:T(8,128)(2,1)} %collective-permute-done.4), kind=kLoop, calls=%fused_computation.7 | loop fusion | flops 26542080 | bytes 7962624 | tf_op jit(solution)/shard_map/concatenate | solution.py:24
  38.8 4.1 %fusion.152 = (bf16[1,6,48,2048]{3,2,1,0:T(8,128)(2,1)S(1)}, bf16[1,6,48,2048]{3,2,1,0:T(8,128)(2,1)}, bf16[1,6,48,2048]{3,2,1,0:T(8,128)(2,1)}, bf16[1,6,48,204...) fusion(bf16[1,18,60,2048]{3,2,1,0:T(8,128)(2,1)S(1)} %fusion.5), kind=kLoop, calls=%fused_computation.100 | loop fusion | bytes 14155776 | tf_op jit(solution)/shard_map/slice | solution.py:63
  42.8 93.8 %all-gather.6.cloned.1.call-done = bf16[1,3,3,2048,256]{4,3,2,1,0:T(8,128)(2,1)} async-done(((bf16[1,3,3,256,256]{4,3,2,1,0:T(8,128)(2,1)}), bf16[1,3,3,2048,256]{4,3,2,1,0:T(8,128)(2,1)}) %all-gather.6.cloned.1.call-update) | async-done | bytes 9437200 | tf_op jit(solution)/shard_map/all_gather | solution.py:59
  136.7 0.0 copy-start.6
  136.7 0.0 copy-start.9
  136.7 2.2 fusion.135
  138.9 0.0 copy-done.6
  138.9 2.4 fusion.136
  141.3 0.0 copy-start.3
  141.3 2.1 fusion.137
  143.5 0.0 copy-done.9
  143.5 0.0 copy-done.3
  143.5 0.0 copy-start.5
  143.5 0.5 fusion.134
  144.0 0.8 copy-done.5
  144.8 0.5 fusion.131
  145.3 0.8 copy-done.4
  146.1 0.0 copy-start.8
  146.1 0.5 fusion.133
  146.5 0.8 copy-done.8
  147.3 0.5 fusion.132
  147.8 0.5 fusion.142
  148.3 0.0 copy-start.10
  148.3 0.5 fusion.44
  148.8 0.4 copy-done.10
  149.2 0.8 fusion.143
  150.0 0.0 all-gather.4.cloned.1.call-update
  150.7 0.0 all-to-all-done
  150.7 6.7 %reshape.187 = bf16[2048,1,6,48]{3,2,1,0:T(8,128)(2,1)} reshape(bf16[8,2,36864]{2,1,0:T(2,128)(2,1)S(1)} %all-to-all-done) | data formatting | bytes 2359296
  157.4 3.8 %copy.13 = bf16[1,6,48,8,256]{4,2,1,3,0:T(8,128)(2,1)S(1)} copy(bf16[1,6,48,8,256]{2,1,4,3,0:T(8,128)(2,1)} %bitcast.250) | data formatting | bytes 2359296 | tf_op jit(solution)/shard_map/all_to_all | solution.py:53
  161.2 38.6 %all-gather.4.cloned.1.call-done = bf16[1,48,48,256]{3,2,0,1:T(8,128)(2,1)} async-done(((bf16[1,6,48,256]{3,2,0,1:T(8,128)(2,1)}), bf16[1,48,48,256]{3,2,0,1:T(8,128)(2,1)}) %all-gather.4.cloned.1.call-update) | async-done | bytes 1179664 | tf_op jit(solution)/shard_map/all_gather | solution.py:68
  199.7 0.0 copy-start
  199.7 1.9 fusion.126
  201.6 0.0 copy-done
  201.6 0.5 fusion.116
  202.1 0.5 fusion.106
  202.6 0.5 fusion.96
  203.1 0.6 fusion.48
  203.7 0.5 fusion.86
  204.2 0.5 fusion.76
  204.8 0.5 fusion.66
  205.3 0.5 fusion.56
  205.8 0.0 copy-start.1
  205.8 0.2 broadcast_multiply_fusion
  206.0 1.1 copy-done.1
  207.1 0.3 convert_subtract_fusion
  207.4 52.4 %conditional.1 = (f32[3,3,256,256]{3,2,1,0:T(8,128)}) conditional(s32[]{:T(128)} %clamp.3, f32[3,3,256,256]{3,2,1,0:T(8,128)S(1)} %convert_subtract_fusion, f32[3,3,256,256]{3,2,1,0:T(8,128)S(1)} %convert_subtract_fusion, f32[3,3,256,256]{3,2,1,0:T(8,128)S(1)} %convert_subtract_fusion, ...), branch_computations={%region_0.1_spmd, %region_1.2_spmd, %region_2.3_spmd, %region_3.4_... | conditional | bytes 9437232 | solution.py:87
  207.5 2.3 collective-permute-start.3
  209.8 50.1 %collective-permute-done.3 = f32[3,3,256,256]{3,2,1,0:T(8,128)} collective-permute-done((f32[3,3,256,256]{3,2,1,0:T(8,128)S(1)}, f32[3,3,256,256]{3,2,1,0:T(8,128)}, u32[]{:S(2)}, u32[]{:S(2)}) %collective-permute-start.3) | collective-permute-done | bytes 2359328 | tf_op jit(solution)/shard_map/cond/branch_3_fun/ppermute | solution.py:15
  259.8 3.0 %fusion.6 = bf16[1,3,3,256,256]{4,3,2,1,0:T(8,128)(2,1)} fusion(f32[3,3,256,256]{3,2,1,0:T(8,128)S(1)} %convert_subtract_fusion, f32[3,3,256,256]{3,2,1,0:T(8,128)} %get-tuple-element.20), kind=kLoop, calls=%fused_computation.18 | loop fusion | flops 1769472 | bytes 5898240 | tf_op jit(solution)/shard_map/broadcast_in_dim | solution.py:89
  (1 shorter events, 0.0 us)
Async XLA Ops:
  6.5 1.3 copy-start.2
  6.5 130.1 %all-gather.6.cloned.1.call-start = ((), (), s32[]{:S(2)}) async-start(), calls=%async_computation.2 | async-start | bytes 10616832 | tf_op jit(solution)/shard_map/all_gather | solution.py:59
  7.8 26.9 %collective-permute-start.4 = (bf16[1,6,48,2048]{3,2,1,0:T(8,128)(2,1)S(1)}, bf16[1,6,48,2048]{3,2,1,0:T(8,128)(2,1)}, u32[]{:S(2)}, u32[]{:S(2)}) collective-permute-start(bf16[1,6,48,2048]{3,2,1,0:T(8,128)(2,1)S(1)} %bitcast.255), channel_id=1, source_target_pairs={{0,1},{1,2},{2,3},{3,4},{4,5},{5,6},{6,7},{8,9},{9,10},{10,11},{11... | collective-permute-start | bytes 3538952 | tf_op jit(solution)/shard_map/ppermute | solution.py:26
  13.2 21.6 %collective-permute-start.5 = (bf16[1,6,48,2048]{3,2,1,0:T(8,128)(2,1)S(1)}, bf16[1,6,48,2048]{3,2,1,0:T(8,128)(2,1)S(1)}, u32[]{:S(2)}, u32[]{:S(2)}) collective-permute-start(bf16[1,6,48,2048]{3,2,1,0:T(8,128)(2,1)S(1)} %bitcast.256), channel_id=1, source_target_pairs={{1,0},{2,1},{3,2},{4,3},{5,4},{6,5},{7,6},{9,8},{10,9},{11,10},{12... | collective-permute-start | bytes 3538952 | tf_op jit(solution)/shard_map/ppermute | solution.py:28
  31.2 119.6 %all-to-all-start = ((bf16[8,2,36864]{2,1,0:T(2,128)(2,1)}), bf16[8,2,36864]{2,1,0:T(2,128)(2,1)S(1)}, u32[]{:S(2)}, u32[]{:S(2)}) async-start(bf16[8,2,36864]{2,1,0:T(2,128)(2,1)} %reshape.186), calls=%async_computation | async-start | bytes 2359296 | tf_op jit(solution)/shard_map/all_to_all | solution.py:53
  34.7 165.0 %all-gather.4.cloned.1.call-start = ((), (), s32[]{:S(2)}) async-start(), calls=%async_computation.1 | async-start | bytes 1327104 | tf_op jit(solution)/shard_map/all_gather | solution.py:68
  34.8 1.1 copy-start.7
  136.7 2.2 copy-start.6
  136.7 6.8 %copy-start.9 = (bf16[1,3,3,2048,256]{4,3,2,1,0:T(8,128)(2,1)S(1)}, bf16[1,3,3,2048,256]{4,3,2,1,0:T(8,128)(2,1)}, u32[]{:S(2)}) copy-start(bf16[1,3,3,2048,256]{4,3,2,1,0:T(8,128)(2,1)} %all-gather.6.cloned.1.call-done) | copy-start | bytes 28311556
  141.3 2.2 copy-start.3
  143.5 1.3 copy-start.5
  144.8 1.3 copy-start.4
  146.1 1.3 copy-start.8
  148.3 0.9 copy-start.10
  199.7 1.9 copy-start
  205.8 1.3 copy-start.1
  207.5 52.4 %collective-permute-start.3 = (f32[3,3,256,256]{3,2,1,0:T(8,128)S(1)}, f32[3,3,256,256]{3,2,1,0:T(8,128)}, u32[]{:S(2)}, u32[]{:S(2)}) collective-permute-start(f32[3,3,256,256]{3,2,1,0:T(8,128)S(1)} %param.3), channel_id=1, source_target_pairs={{448,0},{456,8},{464,16},{472,24},{480,32},{488,40},{496,48},{504,... | collective-permute-start | bytes 7077896 | tf_op jit(solution)/shard_map/cond/branch_3_fun/ppermute | solution.py:15
Sparse Core Ops, SparseCore 0:
  9.4 127.1 all-gather.5
  150.1 49.5 all-gather.3
where the time goes:
time: 273 us; the launch traced here: 270 us
  waiting for transfers between devices  183 us (67%)
  local copies, waits for them, and re-layouts  32.3 us (12%)
  starting transfers between devices  16.9 us (6%)
  matrix products  15.7 us (6%)
  between operations  14.4 us (5%)
  other arithmetic  7.21 us (3%)
    all_gather x1, waiting for transfers between devices, per_device(): piece = lax.all_gather(kernel, 'row', axis=2, tiled=True)  93.8 us
    ppermute x1, waiting for transfers between devices, from_behind(): return lax.ppermute(block, axis, route)  50.1 us
    all_gather x1, waiting for transfers between devices, per_device(): piece = lax.all_gather(slope, 'row', axis=1, tiled=True)  38.6 us
    unnamed x24, local copies, waits for them, and re-layouts  20.2 us
    dot_general x9, matrix products, per_device(): jnp.dot(win, piece[p, q], preferred_element_type=jnp.float32)  9.63 us
    dot_general x9, matrix products, per_device(): lax.dot_general(win, flat, (((0,), (0,)), ((), ())), preferred_element_ty...  6.02 us
    ppermute x1, starting transfers between devices, with_halo(): lax.ppermute(head, axis, [((i + 1) % count, i) for i in range(ends)])  5.69 us
  transfers between devices with their start and end apart: 6, of which 3 were waited for; matrix products, arithmetic and copies ran while one was open for 15% of the time, Pallas kernels for 0%

commit v1 on v0

v1 whole, which is shorter than its diff:
```python
from functools import partial

import jax
import jax.numpy as jnp
from jax import lax
from jax.experimental import pallas as pl
from jax.experimental.pallas import tpu as pltpu
from jax.sharding import PartitionSpec as P

R = 6
HOPS = 4
MESH = pl.DeviceIdType.MESH
FAR_FIRST = (2, 1, 3)


def silu_slope(value):
    sig = jax.nn.sigmoid(value)
    return sig * (1.0 + value * (1.0 - sig))


def step_kernel(
    off, cols, scale_in,
    f_ref, w_ref, u_ref, rate_ref, out_ref,
    fcat, wv, uv, pair_tx, pair_rx, sum_tx, sum_rx, slopes, stepped, peer_tx, peer_rx,
    load_sem, move_tx, move_rx, pair_txs, pair_rxs, sum_txs, sum_rxs,
    ring_txs, ring_rxs, fwd_txs, fwd_rxs, peer_txs, peer_rxs,
):
    rows, share = uv.shape[0], wv.shape[1]
    count = lax.axis_size("row")
    chips = count // 2
    reps = lax.axis_size("rep")
    me = lax.axis_index("row")
    rep = lax.axis_index("rep")
    z, c = lax.div(me, 2), lax.rem(me, 2)
    other = 1 - c
    mate = 2 * z + other
    ahead = lax.rem(rep + off, reps)
    behind = lax.rem(rep + reps - off, reps)

    def up(d):
        return lax.rem(z + d, chips)

    def down(d):
        return lax.rem(z + chips - d, chips)

    def rows_of(j):
        return pl.ds(pl.multiple_of(j * rows, rows), rows)

    mid = pl.ds(share, share)

    def load(k, src, dst):
        return pltpu.make_async_copy(src, dst, load_sem.at[k])

    def columns_for(t):
        return f_ref.at[:, pl.ds(pl.multiple_of(t * share, share), share)]

    loads = [
        load(0, columns_for(me), fcat.at[rows_of(me + 1), mid]),
        load(1, w_ref, wv),
        load(2, u_ref, uv),
    ]
    for one in loads:
        one.start()

    barrier = pltpu.get_barrier_semaphore()
    for k in range(1, count):
        to = lax.rem(me + k, count)
        pl.semaphore_signal(barrier, inc=1, device_id={"row": to}, device_id_type=MESH)
    for to in (ahead, behind):
        pl.semaphore_signal(barrier, inc=1, device_id={"rep": to}, device_id_type=MESH)
    pl.semaphore_wait(barrier, count + 1)

    def move(dz, dc):
        to = 2 * up(dz) + lax.rem(c + dc, 2)
        k = 2 * dz + dc
        return pltpu.make_async_remote_copy(
            columns_for(to), fcat.at[rows_of(me + 1), mid],
            move_tx.at[k], move_rx.at[k], device_id={"row": to}, device_id_type=MESH,
        )

    def moved(dz, dc):
        src = 2 * down(dz) + lax.rem(c + dc, 2)
        k = 2 * dz + dc
        copy = pltpu.make_async_remote_copy(
            columns_for(src), fcat.at[rows_of(src + 1), mid],
            move_tx.at[k], move_rx.at[k], device_id={"row": src}, device_id_type=MESH,
        )
        return src, copy

    order = [(dz, dc) for dz in FAR_FIRST for dc in (0, 1)] + [(0, 1)]
    for dz, dc in order:
        move(dz, dc).start()

    edge = jnp.zeros((rows, 3 * share), fcat.dtype)
    fcat[pl.ds(0, rows), :] = edge
    fcat[pl.ds((count + 1) * rows, rows), :] = edge

    col = lax.rem(lax.broadcasted_iota(jnp.int32, (rows, share), 0), cols)

    def shift(j):
        at = rows_of(j + 1)
        x = fcat[at, pl.ds(share, share)].astype(jnp.float32)
        left = jnp.where(col < R, 0.0, pltpu.roll(x, R, 0))
        right = jnp.where(col >= cols - R, 0.0, pltpu.roll(x, rows - R, 0))
        fcat[at, pl.ds(0, share)] = left.astype(fcat.dtype)
        fcat[at, pl.ds(2 * share, share)] = right.astype(fcat.dtype)

    loads[0].wait()
    shift(me)
    for dz, dc in [(0, 1)] + order[:-1]:
        src, copy = moved(dz, dc)
        copy.wait_recv()
        shift(src)
    loads[1].wait()
    loads[2].wait()

    def partial_sum(j):
        total = None
        for p in range(3):
            term = jnp.dot(
                fcat[rows_of(j + p), :], wv[pl.ds(p * 3 * share, 3 * share), :],
                preferred_element_type=jnp.float32,
            )
            total = term if total is None else total + term
        return total

    def pair(dz):
        return pltpu.make_async_remote_copy(
            pair_tx.at[dz], pair_rx.at[dz], pair_txs.at[dz], pair_rxs.at[dz],
            device_id={"row": mate}, device_id_type=MESH,
        )

    def give(dz, ring):
        tx, rx = (sum_txs, sum_rxs)
        return pltpu.make_async_remote_copy(
            sum_tx.at[dz - 1], sum_rx.at[dz - 1], tx.at[dz], rx.at[dz],
            device_id={"row": 2 * up(dz) + c}, device_id_type=MESH,
        )

    for dz in FAR_FIRST + (0,):
        pair_tx[dz] = partial_sum(2 * up(dz) + other).astype(pair_tx.dtype)
        pair(dz).start()
    for dz in FAR_FIRST:
        mine = partial_sum(2 * up(dz) + c)
        pair(dz).wait_recv()
        sum_tx[dz - 1] = (mine + pair_rx[dz].astype(jnp.float32)).astype(sum_tx.dtype)
        give(dz, 0).start()
    pre = partial_sum(me)
    pair(0).wait_recv()
    pre = pre + pair_rx[0].astype(jnp.float32)
    for dz in FAR_FIRST:
        give(dz, 0).wait_recv()
        pre = pre + sum_rx[dz - 1].astype(jnp.float32)
    pre = pre * scale_in
    slopes[rows_of(me), :] = (uv[...].astype(jnp.float32) * silu_slope(pre)).astype(slopes.dtype)

    def spread(dz):
        at = slopes.at[rows_of(me)]
        return pltpu.make_async_remote_copy(
            at, at, ring_txs.at[dz], ring_rxs.at[dz],
            device_id={"row": 2 * up(dz) + c}, device_id_type=MESH,
        )

    def arrived(dz):
        src = 2 * down(dz) + c
        at = slopes.at[rows_of(src)]
        return pltpu.make_async_remote_copy(
            at, at, ring_txs.at[dz], ring_rxs.at[dz],
            device_id={"row": src}, device_id_type=MESH,
        )

    def hand(dz, core):
        at = slopes.at[rows_of(2 * down(dz) + core)]
        return pltpu.make_async_remote_copy(
            at, at, fwd_txs.at[dz], fwd_rxs.at[dz],
            device_id={"row": mate}, device_id_type=MESH,
        )

    for dz in FAR_FIRST:
        spread(dz).start()
    hand(0, c).start()
    for dz in FAR_FIRST:
        arrived(dz).wait_recv()
        hand(dz, c).start()
    for dz in (0,) + FAR_FIRST:
        hand(dz, other).wait_recv()

    rate = rate_ref[0]

    def gossip(p):
        return pltpu.make_async_remote_copy(
            peer_tx.at[p], peer_rx.at[p], peer_txs.at[p], peer_rxs.at[p],
            device_id={"rep": ahead}, device_id_type=MESH,
        )

    height = count * rows
    for p in range(3):
        grad = lax.dot_general(
            fcat[pl.ds(p * rows, height), :], slopes[...],
            (((0,), (0,)), ((), ())), preferred_element_type=jnp.float32,
        )
        new = wv[pl.ds(p * 3 * share, 3 * share), :].astype(jnp.float32) - rate * grad
        stepped[p] = new
        peer_tx[p] = new.astype(peer_tx.dtype)
        gossip(p).start()
    for p in range(3):
        gossip(p).wait_recv()
        out_ref[pl.ds(p * 3 * share, 3 * share), :] = (
            (stepped[p] + peer_rx[p].astype(jnp.float32)) * 0.5
        ).astype(out_ref.dtype)

    for dz, dc in order:
        move(dz, dc).wait_send()
    for dz in range(chips):
        pair(dz).wait_send()
        hand(dz, c).wait_send()
    for dz in FAR_FIRST:
        give(dz, 0).wait_send()
        spread(dz).wait_send()
    for p in range(3):
        gossip(p).wait_send()


def run_step(hop, f, w, u, rate, cols, scale_in):
    rows, chans = f.shape
    taps, outs = w.shape
    count = chans // (taps // 9)
    chips = count // 2
    share = taps // 9
    bf, f32 = jnp.bfloat16, jnp.float32
    dma = pltpu.SemaphoreType.DMA
    anywhere = pl.BlockSpec(memory_space=pl.ANY)
    return pl.pallas_call(
        partial(step_kernel, 1 << hop, cols, scale_in),
        out_shape=jax.ShapeDtypeStruct((taps, outs), bf),
        in_specs=[anywhere, anywhere, anywhere, pl.BlockSpec(memory_space=pltpu.SMEM)],
        out_specs=pl.BlockSpec(memory_space=pltpu.VMEM),
        scratch_shapes=[
            pltpu.VMEM(((count + 2) * rows, 3 * share), bf),
            pltpu.VMEM((taps, outs), bf),
            pltpu.VMEM((rows, outs), bf),
            pltpu.VMEM((chips, rows, outs), f32),
            pltpu.VMEM((chips, rows, outs), f32),
            pltpu.VMEM((chips - 1, rows, outs), bf),
            pltpu.VMEM((chips - 1, rows, outs), bf),
            pltpu.VMEM((count * rows, outs), bf),
            pltpu.VMEM((3, 3 * share, outs), f32),
            pltpu.VMEM((3, 3 * share, outs), bf),
            pltpu.VMEM((3, 3 * share, outs), bf),
            dma((3,)),
            dma((count,)), dma((count,)),
            dma((chips,)), dma((chips,)),
            dma((chips,)), dma((chips,)),
            dma((chips,)), dma((chips,)),
            dma((chips,)), dma((chips,)),
            dma((3,)), dma((3,)),
        ],
        compiler_params=pltpu.CompilerParams(
            collective_id=hop, has_side_effects=True, vmem_limit_bytes=48 << 20
        ),
    )(f, w, u, rate)


def per_device(features, weights, upstream, step_index):
    _, batch, rows_dev, cols, chans_in = features.shape
    share, chans_out = weights.shape[3:]
    rows_all = rows_dev * lax.axis_size("row")
    scale_in = 1.0 / (9 * chans_in) ** 0.5
    scale_grad = 1.0 / jnp.sqrt(jnp.float32(batch * rows_all * cols))
    rate = scale_grad / jnp.sqrt(1.0 + step_index.astype(jnp.float32) / 1024.0)
    f = features.reshape(rows_dev * cols, chans_in)
    w = weights.reshape(9 * share, chans_out)
    u = upstream.reshape(rows_dev * cols, chans_out)
    branches = [partial(run_step, hop, cols=cols, scale_in=scale_in) for hop in range(HOPS)]
    out = lax.switch(step_index[0] % HOPS, branches, f, w, u, rate)
    return out.reshape(weights.shape)


def solution(mesh):
    in_specs = (
        P("rep", None, "row", None, None),
        P("rep", None, None, "row", None),
        P("rep", None, "row", None, None),
        P(),
    )
    out_specs = P("rep", None, None, "row", None)
    return jax.shard_map(
        per_device, mesh=mesh, in_specs=in_specs, out_specs=out_specs, check_vma=False
    )
```

time: 273 us -> 99.2 us (0.36); the launches traced: 270 us -> 99.1 us
  waiting for transfers between devices: 183 us -> 0 us
  Pallas kernels: 0 us -> 96.6 us
  local copies, waits for them, and re-layouts: 32.3 us -> 1.02 us
  starting transfers between devices: 16.9 us -> 0 us
  matrix products: 15.7 us -> 0 us
  between operations: 14.4 us -> 0.68 us
  other arithmetic: 7.21 us -> 0 us
    all_gather x2 -> x0, waiting for transfers between devices: 132 us -> none  [the longest x1 93.8 us: per_device(): piece = lax.all_gather(kernel, 'row', axis=2, tiled=True)]
    pallas_call x0 -> x1, Pallas kernels: none -> 96.6 us  [run_step(): pl.pallas_call(partial(step_kernel, 1 << hop, cols, scale_in), out_shape=...]
    ppermute x3 -> x0, waiting for transfers between devices: 50.1 us -> none  [the longest x1 50.1 us: from_behind(): return lax.ppermute(block, axis, route)]
    unnamed x24 -> x1, local copies, waits for them, and re-layouts: 20.2 us -> 1.02 us
    dot_general x18 -> x0, matrix products: 15.7 us -> none  [the longest x9 9.63 us: per_device(): jnp.dot(win, piece[p, q], preferred_element_type=jnp.float32)]
    ppermute x3 -> x0, starting transfers between devices: 13.4 us -> none  [the longest x1 5.69 us: with_halo(): lax.ppermute(head, axis, [((i + 1) % count, i) for i in range(ends)])]
    squeeze x1 -> x0, local copies, waits for them, and re-layouts: 4.22 us -> none  [per_device(): feats = features[0]]
    slice x1 -> x0, local copies, waits for them, and re-layouts: 4.06 us -> none  [per_device(): win = padded[:, p * R:p * R + rows_dev, q * R:q * R + cols, :]]
  transfers between devices with their start and end apart: 6 -> 0, of which waited for: 3 -> 0; matrix products, arithmetic and copies ran while one was open for 15% -> 0% of each run, Pallas kernels for 0% -> 0%
where the time goes in v1:
time: 99.2 us; the launch traced here: 99.1 us
  Pallas kernels  96.6 us (97%)
  local copies, waits for them, and re-layouts  1.02 us (1%)
    pallas_call x1, Pallas kernels, run_step(): pl.pallas_call(partial(step_kernel, 1 << hop, cols, scale_in), out_shape=...  96.6 us

profile of v1, /device:TPU:1, one launch (start us, length us, event | category | flops | bytes accessed | tf_op | source)
XLA Modules:
  0.0 99.1 jit_solution(17255670430438127037)
XLA Ops:
  0.7 97.4 %conditional.1 = (bf16[1,3,3,256,256]{4,3,2,1,0:T(8,128)(2,1)S(1)}) conditional(s32[]{:T(128)} %clamp.3, (bf16[1,1,6,48,2048]{4,3,2,1,0:T(8,128)(2,1)}, bf16[1,3,3,256,256]{4,3,2,1,0:T(8,128)(2,1)}, bf16[1,1,6,48,256]{4,3,2,1,0:T(8,128)(2,1)}, f32[1]{0:T(128)}) %tuple.56, (bf16[1,1,6,48,2048]{4,3,2,1,0:T(8,128)(2,1)}, ...), branch_computations={%region_0.1_spmd, %region_1.2_spmd, %region_2.3_spmd, %region_3.4_... | conditional | flops 3 | bytes 52 | solution.py:275
  0.9 96.6 %branch_1_fun.2 = bf16[2304,256]{1,0:T(8,128)(2,1)S(1)} custom-call(bf16[288,2048]{1,0:T(8,128)(2,1)} %bitcast.21, bf16[2304,256]{1,0:T(8,128)(2,1)} %bitcast.25, bf16[288,256]{1,0:T(8,128)(2,1)} %bitcast.33, f32[1]{0:T(128)S(6)} %div.9.rate_ref), custom_call_target="tpu_custom_call" | custom-call | tf_op jit(solution)/shard_map/cond/branch_1_fun/pallas_call | solution.py:233
  98.1 1.0 %copy.27 = bf16[1,3,3,256,256]{4,3,2,1,0:T(8,128)(2,1)} copy(bf16[1,3,3,256,256]{4,3,2,1,0:T(8,128)(2,1)S(1)} %get-tuple-element.131) | data formatting | bytes 2359296
